TPU v7x, 256 devices: a whole 4x4x8 slice. The times are simulated.
256 devices in a mesh: freq: 4 (over z_hi), rows: 64 (over y, z_lo, x, core).
Axes of the slice: x: 4, y: 4, z: 8 (z_hi: 4, z_lo: 2; z = z_hi * 2 + z_lo), core: 2. Of those that a mesh axis runs over, the one named last changes fastest.
Arguments:
- reflection: bfloat16 [32, 2, 2048, 2048], P('freq', None, 'rows'), may hold values from -0.25 to 0.25
- focus_direct: bfloat16 [32, 2048, 128], P('freq', 'rows'), may hold values from -6 to 6
- onsets: int32 [2048, 64], P('rows'), may hold values from 8 to 63
Outputs:
- focus_plus: bfloat16 [32, 2048, 128], P('freq', 'rows')
- focus_minus: bfloat16 [32, 2048, 128], P('freq', 'rows')
All inputs are finite; a program needn't handle non-finite values.
Results may differ from a plain program's by a relative error of at most 0.015.
Values may be sent and summed in bfloat16 or wider, within the bound.
A program may use at most 128 MiB of HBM per device.

v0:
```python
import math

import jax
import jax.numpy as jnp
from jax import lax
from jax.sharding import PartitionSpec as P

NT = 128
ITERS = 2


def spectra_tables(freq_total, temporal_ticks):
    spectral_axis_values = jnp.arange(1, freq_total + 1, dtype=jnp.int32)
    temporal_moments = jnp.arange(temporal_ticks, dtype=jnp.int32)
    rotation_angles_matrix = (
        temporal_moments[:, None] * spectral_axis_values[None, :] % temporal_ticks
    )
    angles = rotation_angles_matrix.astype(jnp.float32) * jnp.float32(
        2.0 * math.pi / temporal_ticks
    )
    return (jnp.cos(angles), jnp.sin(angles))


def mask_table(gate_starting_tiles, temporal_ticks):
    temporal_moments = jnp.arange(temporal_ticks, dtype=jnp.int32)[:, None, None]
    inside_gate_mask = (temporal_moments < gate_starting_tiles[None]) | (
        temporal_ticks - temporal_moments < gate_starting_tiles[None]
    )
    return inside_gate_mask.astype(jnp.float32)


def window_spectra(fourier_coefficients, mask, cosinus_factor, sine):
    temporal_ticks = cosinus_factor.shape[0]
    half_cols = fourier_coefficients.shape[-1] // 2
    values = fourier_coefficients.astype(jnp.float32)
    real_part = values[..., :half_cols]
    imag_part = values[..., half_cols:]
    highest_mode = lax.Precision.HIGHEST
    traces = 2.0 * (
        jnp.einsum("tk,krp->trp", cosinus_factor, real_part, precision=highest_mode)
        - jnp.einsum("tk,krp->trp", sine, imag_part, precision=highest_mode)
    )
    kept_traces = traces * mask
    new_real = (
        jnp.einsum("tk,trp->krp", cosinus_factor, kept_traces, precision=highest_mode)
        / temporal_ticks
    )
    new_imag = (
        -jnp.einsum("tk,trp->krp", sine, kept_traces, precision=highest_mode) / temporal_ticks
    )
    return jnp.concatenate([new_real, new_imag], axis=-1)


def forward_combine(with_real, with_imag, half_cols):
    real_out = with_real[..., :half_cols] - with_imag[..., half_cols:]
    imag_out = with_real[..., half_cols:] + with_imag[..., :half_cols]
    return jnp.concatenate([real_out, imag_out], axis=-1)


def adjoint_combine(with_real, with_imag, half_cols):
    real_out = with_real[..., :half_cols] + with_imag[..., half_cols:]
    imag_out = with_real[..., half_cols:] - with_imag[..., :half_cols]
    return jnp.concatenate([real_out, imag_out], axis=-1)


def local(reflection, focus_direct, onsets):
    freq_count = lax.axis_size("freq")
    rows_count = lax.axis_size("rows")
    freq_index = lax.axis_index("freq")
    freq_local = reflection.shape[0]
    rows_dev = reflection.shape[2]
    quarter_rows = rows_dev // freq_count
    freq_total = freq_local * freq_count
    columns_all = focus_direct.shape[2]
    half_cols = columns_all // 2
    cosinus_factor, sine = spectra_tables(freq_total, NT)
    gate_starting_tiles = lax.dynamic_slice_in_dim(
        onsets, freq_index * quarter_rows, quarter_rows, 0
    )
    mask = mask_table(gate_starting_tiles, NT)
    broad_direct_arrival = focus_direct.astype(jnp.float32)
    plus = focus_direct
    minus = focus_direct
    for step in range(ITERS):
        gathered = lax.all_gather(plus, "rows", axis=1, tiled=True)
        phase_product = jnp.einsum(
            "fcrs,fsq->fcrq", reflection, gathered, preferred_element_type=jnp.float32
        )
        convolved = forward_combine(phase_product[:, 0], phase_product[:, 1], half_cols).astype(
            jnp.bfloat16
        )
        conv_traces = lax.all_to_all(convolved, "freq", split_axis=1, concat_axis=0, tiled=True)
        minus_traces = window_spectra(conv_traces, mask, cosinus_factor, sine).astype(jnp.bfloat16)
        minus = lax.all_to_all(minus_traces, "freq", split_axis=0, concat_axis=1, tiled=True)
        terms = jnp.einsum("fcrs,frq->fcsq", reflection, minus, preferred_element_type=jnp.float32)
        partial_terms = adjoint_combine(terms[:, 0], terms[:, 1], half_cols)
        blocks = partial_terms.reshape(
            freq_local, rows_count, freq_count, quarter_rows, columns_all
        )
        moved = lax.all_to_all(
            blocks.astype(jnp.bfloat16), "freq", split_axis=2, concat_axis=0, tiled=True
        ).astype(blocks.dtype)
        moved = moved.reshape(freq_total, rows_count * quarter_rows, columns_all)
        corr_traces = lax.psum_scatter(moved, "rows", scatter_dimension=1, tiled=True)
        plus_traces = window_spectra(corr_traces, mask, cosinus_factor, sine)
        plus_back = lax.all_to_all(
            plus_traces.astype(jnp.bfloat16), "freq", split_axis=0, concat_axis=1, tiled=True
        ).astype(plus_traces.dtype)
        plus = (broad_direct_arrival + plus_back).astype(jnp.bfloat16)
    return (plus, minus)


def solution(mesh):
    in_specs = (P("freq", None, "rows", None), P("freq", "rows", None), P("rows", None))
    out_specs = (P("freq", "rows", None), P("freq", "rows", None))
    return jax.shard_map(local, mesh=mesh, in_specs=in_specs, out_specs=out_specs, check_vma=False)
```

profile of v0, /device:TPU:1, one launch (start us, length us, event | category | flops | bytes accessed | tf_op | source)
XLA Modules:
  0.0 1182.9 jit_solution(14768019870218236331)
XLA Ops:
  8.6 113.9 %all-gather.3.cloned.1.call-done = bf16[8,2048,128]{2,1,0:T(8,128)(2,1)} async-done(((bf16[8,32,128]{2,1,0:T(8,128)(2,1)}), bf16[8,2048,128]{2,1,0:T(8,128)(2,1)}) %all-gather.3.cloned.1.call-update) | async-done | bytes 4194320 | tf_op jit(solution)/shard_map/all_gather | solution.py:85
  122.6 3.1 fusion.6
  126.6 6.1 all-to-all-start
  132.7 6.9 all-to-all-done
  142.4 9.3 all_to_all.108
  151.8 2.4 convolution_bitcast_fusion.1
  154.1 6.3 slice_bitcast_fusion.3
  160.4 6.5 fusion.3
  167.0 2.5 pad_maximum_fusion
  169.5 6.5 copy.37
  176.0 3.3 copy.38
  179.4 94.6 %all_to_all.109 = bf16[8,64,4,8,128]{4,3,1,0,2:T(8,128)(2,1)S(1)} all-to-all(bf16[8,64,4,8,128]{4,3,1,0,2:T(8,128)(2,1)S(1)} %copy.38), channel_id=1, replica_groups=mesh['freq'=4,'rows'=64] {'freq'}, dimensions={2} | all-to-all | bytes 8388608 | tf_op jit(solution)/shard_map/all_to_all | solution.py:100
  275.0 8.1 copy.39
  283.2 294.9 %reduce-scatter.3.cloned.1.call-done = f32[32,8,128]{2,0,1:T(8,128)} async-done(((f32[32,512,128]{2,0,1:T(8,128)}), f32[32,8,128]{2,0,1:T(8,128)}) %reduce-scatter.3.cloned.1.call-update) | async-done | bytes 131088 | tf_op jit(solution)/shard_map/reduce_scatter | solution.py:104
  579.7 1.6 fusion.14
  583.2 12.7 %all_to_all.110 = bf16[32,8,128]{2,1,0:T(8,128)(2,1)S(1)} all-to-all(bf16[32,8,128]{2,1,0:T(8,128)(2,1)S(1)} %copy.40), channel_id=1, replica_groups=mesh['freq'=4,'rows'=64] {'freq'}, dimensions={0} | all-to-all | bytes 131072 | tf_op jit(solution)/shard_map/all_to_all | solution.py:106
  596.6 106.3 %all-gather.5.cloned.1.call-done = bf16[8,2048,128]{2,1,0:T(8,128)(2,1)} async-done(((bf16[8,32,128]{2,1,0:T(8,128)(2,1)}), bf16[8,2048,128]{2,1,0:T(8,128)(2,1)}) %all-gather.5.cloned.1.call-update) | async-done | bytes 4194320 | tf_op jit(solution)/shard_map/all_gather | solution.py:85
  702.9 3.0 fusion.8
  706.2 12.8 %all_to_all.111 = bf16[8,32,128]{2,0,1:T(8,128)(2,1)S(1)} all-to-all(bf16[8,32,128]{2,0,1:T(8,128)(2,1)S(1)} %copy.43), channel_id=1, replica_groups=mesh['freq'=4,'rows'=64] {'freq'}, dimensions={1} | all-to-all | bytes 131072 | tf_op jit(solution)/shard_map/all_to_all | solution.py:92
  721.8 9.3 all_to_all.112
  731.2 2.4 convolution_bitcast_fusion
  733.6 6.3 slice_bitcast_fusion.1
  739.9 6.5 fusion.1
  746.4 2.5 pad_maximum_fusion.1
  748.9 6.5 copy.48
  755.5 3.3 copy.49
  758.8 95.3 %all_to_all.113 = bf16[8,64,4,8,128]{4,3,1,0,2:T(8,128)(2,1)S(1)} all-to-all(bf16[8,64,4,8,128]{4,3,1,0,2:T(8,128)(2,1)S(1)} %copy.49), channel_id=1, replica_groups=mesh['freq'=4,'rows'=64] {'freq'}, dimensions={2} | all-to-all | bytes 8388608 | tf_op jit(solution)/shard_map/all_to_all | solution.py:100
  855.1 8.1 copy.50
  863.2 293.3 %reduce-scatter.5.cloned.1.call-done = f32[32,8,128]{2,0,1:T(8,128)} async-done(((f32[32,512,128]{2,0,1:T(8,128)}), f32[32,8,128]{2,0,1:T(8,128)}) %reduce-scatter.5.cloned.1.call-update) | async-done | bytes 131088 | tf_op jit(solution)/shard_map/reduce_scatter | solution.py:104
  1158.1 1.6 fusion.12
  1162.2 6.4 all-to-all-start.7
  1169.3 6.4 all-to-all-done.7
  (54 shorter events, 19.9 us)
Async XLA Ops:
  7.2 115.4 %copy-start = (bf16[8,2,32,2048]{3,2,1,0:T(8,128)(2,1)S(1)}, bf16[8,2,32,2048]{3,2,1,0:T(8,128)(2,1)}, u32[]{:S(2)}) copy-start(bf16[8,2,32,2048]{3,2,1,0:T(8,128)(2,1)} %param.3) | copy-start | bytes 6291460
  7.2 115.4 %all-gather.3.cloned.1.call-start = ((), (), s32[]{:S(2)}) async-start(), calls=%async_computation.10 | async-start | bytes 4259840 | tf_op jit(solution)/shard_map/all_gather | solution.py:85
  126.6 12.9 %all-to-all-start = ((bf16[8,32,128]{2,0,1:T(8,128)(2,1)}), bf16[8,32,128]{2,0,1:T(8,128)(2,1)S(1)}, u32[]{:S(2)}, u32[]{:S(2)}) async-start(bf16[8,32,128]{2,0,1:T(8,128)(2,1)} %copy.32), calls=%async_computation | async-start | bytes 131072 | tf_op jit(solution)/shard_map/all_to_all | solution.py:92
  132.6 445.5 %reduce-scatter.3.cloned.1.call-start = ((), (), s32[]{:S(2)}) async-start(), calls=%async_computation.11 | async-start | bytes 8519680 | tf_op jit(solution)/shard_map/reduce_scatter | solution.py:104
  283.1 312.8 %copy-start.2 = (bf16[8,32,128]{2,1,0:T(8,128)(2,1)S(1)}, bf16[8,32,128]{2,1,0:T(8,128)(2,1)}, u32[]{:S(2)}) copy-start(bf16[8,32,128]{2,1,0:T(8,128)(2,1)} %param.4) | copy-start | bytes 196612
  283.1 419.8 %all-gather.5.cloned.1.call-start = ((), (), s32[]{:S(2)}) async-start(), calls=%async_computation.12 | async-start | bytes 4259840 | tf_op jit(solution)/shard_map/all_gather | solution.py:85
  596.6 559.9 %reduce-scatter.5.cloned.1.call-start = ((), (), s32[]{:S(2)}) async-start(), calls=%async_computation.13 | async-start | bytes 8519680 | tf_op jit(solution)/shard_map/reduce_scatter | solution.py:104
  863.2 313.2 %copy-start.1 = (bf16[8,2,32,2048]{3,2,1,0:T(8,128)(2,1)S(1)}, bf16[8,2,32,2048]{3,2,1,0:T(8,128)(2,1)}, u32[]{:S(2)}) copy-start(bf16[8,2,32,2048]{3,2,1,0:T(8,128)(2,1)} %param.3) | copy-start | bytes 6291460
  1162.2 13.5 %all-to-all-start.7 = ((bf16[32,8,128]{2,1,0:T(8,128)(2,1)}), bf16[32,8,128]{2,1,0:T(8,128)(2,1)S(1)}, u32[]{:S(2)}, u32[]{:S(2)}) async-start(bf16[32,8,128]{2,1,0:T(8,128)(2,1)} %copy.51), calls=%async_computation.9 | async-start | bytes 131072 | tf_op jit(solution)/shard_map/all_to_all | solution.py:106
Sparse Core Ops, SparseCore 0:
  9.9 112.6 all-gather.2
  283.3 294.8 reduce-scatter.2
  596.7 106.1 all-gather.4
  863.3 293.1 reduce-scatter.4
where the time goes:
time: 1190 us; the launch traced here: 1180 us
  waiting for transfers between devices  823 us (69%)
  blocking collectives  234 us (20%)
  local copies, waits for them, and re-layouts  51.4 us (4%)
  matrix products  26 us (2%)
  other arithmetic  22.2 us (2%)
  between operations  14.1 us (1%)
  starting transfers between devices  12.6 us (1%)
    reduce_scatter x2, waiting for transfers between devices, local(): lax.psum_scatter(moved, 'rows', scatter_dimension=1, tiled=True)  588 us
    all_gather x2, waiting for transfers between devices, local(): gathered = lax.all_gather(plus, 'rows', axis=1, tiled=True)  220 us
    all_to_all x2, blocking collectives, local(): lax.all_to_all(blocks.astype(jnp.bfloat16), 'freq', split_axis=2, concat_...  190 us
  transfers between devices with their start and end apart: 6, of which 6 were waited for; matrix products, arithmetic and copies ran while one was open for 0% of the time, Pallas kernels for 0%

commit v1 on v0

v1 whole, which is shorter than its diff:
```python
import math

import jax
import jax.numpy as jnp
import numpy as np
from jax import lax
from jax.experimental import pallas as pl
from jax.experimental.pallas import tpu as pltpu
from jax.sharding import PartitionSpec as P

NT = 128
ITERS = 2
MESH = pl.DeviceIdType.MESH
BF = jnp.bfloat16
F32 = jnp.float32


def window_tables():
    t = np.arange(64)[:, None]
    k = np.arange(1, 33)[None, :]
    ang = 2.0 * np.pi * ((t * k) % NT) / NT
    parts = np.stack([np.cos(ang), np.sin(ang)])
    eye = np.eye(8)
    first = np.einsum("ctf,rs->trcfs", parts, eye).reshape(512, 512)
    weight = np.where(np.arange(64) == 0, 2.0, 4.0) / NT
    back = parts * weight[None, :, None]
    second = np.einsum("ctgf,rs->gcfrts", back.reshape(2, 64, 4, 8), eye).reshape(4, 128, 512)
    return first.astype(jnp.bfloat16), second.astype(jnp.bfloat16)


def turned(block, sign):
    real, imag = block[:, :64], block[:, 64:]
    if sign > 0:
        return jnp.concatenate([-imag, real], axis=1)
    return jnp.concatenate([imag, -real], axis=1)


def kernel(refl, direct, onsets, first, second, plus_out, minus_out,
           rsend, rblk, rtrans, plus, pblk, s1, r1, xf1, minus, mblk, s2, r2, xf2, onw,
           rsnd, rrcv, ssem, rsem):
    fme = lax.axis_index("freq")
    row = lax.axis_index("rows")
    c = lax.rem(row, 2)
    x = lax.rem(row // 2, 4)
    z = lax.rem(row // 8, 2)
    y = row // 16
    zero = c == 0
    u = jnp.where(zero, y, x)
    v = jnp.where(zero, x, y)

    def rows(y, z, x, c):
        return ((y * 2 + z) * 4 + x) * 2 + c

    def wrap(a):
        return lax.rem(a + 8, 4)

    def ring_u(du, dz):
        up, zp = wrap(u + du), lax.rem(z + dz, 2)
        return (fme, jnp.where(zero, rows(up, zp, x, c), rows(y, zp, up, c)))

    def to_ring(d, cp):
        return (fme, rows(y, z, wrap(x + d), 0) if cp == 0 else rows(wrap(y + d), z, x, 1))

    def on_ring(d, cp):
        vp = wrap(v + d)
        return (fme, jnp.where(zero, rows(y, z, vp, cp), rows(vp, z, x, cp)))

    partner = (fme, rows(y, z, x, 1 - c))

    def freq_on(d):
        return (wrap(fme + d), row)

    bar = pltpu.get_barrier_semaphore()
    peers = [partner]
    peers += [ring_u(du, dz) for du in range(4) for dz in range(2) if (du, dz) != (0, 0)]
    peers += [to_ring(d, cp) for d in range(1, 4) for cp in range(2)]
    peers += [on_ring(d, cp) for d in range(1, 4) for cp in range(2)]
    peers += [freq_on(d) for d in range(1, 4)]
    for q in peers:
        pl.semaphore_signal(bar, inc=1, device_id=q, device_id_type=MESH)

    def copy(src, dst, send, recv, device):
        return pltpu.make_async_remote_copy(
            src_ref=src, dst_ref=dst, send_sem=send, recv_sem=recv, device_id=device, device_id_type=MESH)

    def pieces(cp, w):
        if cp == 0:
            return [(k * 256 + w * 64) for k in range(8)]
        return [((w * 2 + k % 2) * 256 + (k // 2) * 64 + 32) for k in range(8)]

    def arrange(cp):
        def step(f, carry):
            block = refl[f].reshape(64, 2048)
            for w in range(4):
                out = jnp.concatenate([block[:, p:p + 32] for p in pieces(cp, w)], axis=1)
                rsend[cp * 4 + w, f] = out.reshape(2, 32, 256)
            return carry
        lax.fori_loop(0, 8, step, 0)

    mine = v * 2 + c

    def send_reflection(d, cp):
        w = wrap((x if cp == 0 else y) + d)
        slot = (x if cp == 0 else y) * 2 + c
        return copy(rsend.at[cp * 4 + w], rblk.at[:, :, pl.ds(pl.multiple_of(slot * 32, 32), 32), :],
                    rsnd.at[d * 2 + cp], rrcv.at[d * 2 + c], to_ring(d, cp))

    def partner_reflection():
        other = 1 - c
        w = jnp.where(zero, y, x)
        slot = jnp.where(zero, y, x) * 2 + c
        return copy(rsend.at[other * 4 + w], rblk.at[:, :, pl.ds(pl.multiple_of(slot * 32, 32), 32), :],
                    rsnd.at[0], rrcv.at[c], partner)

    def recv_reflection(d, cs):
        slot = wrap(v - d) * 2 + cs
        return copy(rsend.at[0], rblk.at[:, :, pl.ds(pl.multiple_of(slot * 32, 32), 32), :],
                    rsnd.at[0], rrcv.at[d * 2 + cs], partner)

    arrange(0)
    plus[0] = direct[...]
    pl.semaphore_wait(bar, len(peers))

    def gather_plus(it, du, dz):
        slot = u * 2 + z
        i = du * 2 + dz
        return copy(plus.at[it], pblk.at[it, :, pl.ds(pl.multiple_of(slot * 32, 32), 32), :],
                    ssem.at[it, i], rsem.at[it, i], ring_u(du, dz))

    def recv_plus(it, du, dz):
        slot = wrap(u - du) * 2 + lax.rem(z + dz, 2)
        i = du * 2 + dz
        return copy(plus.at[it], pblk.at[it, :, pl.ds(pl.multiple_of(slot * 32, 32), 32), :],
                    ssem.at[it, i], rsem.at[it, i], ring_u(du, dz))

    around = [(du, dz) for du in range(4) for dz in range(2) if (du, dz) != (0, 0)]

    for d in (2, 1, 3):
        send_reflection(d, 0).start()
    arrange(1)
    for d in (2, 1, 3):
        send_reflection(d, 1).start()
    partner_reflection().start()
    for du, dz in around:
        gather_plus(0, du, dz).start()
    rblk[:, :, pl.ds(pl.multiple_of(mine * 32, 32), 32), :] = rsend[c * 4 + v]

    on = onsets[...]
    for h in range(2):
        low, high = on[h * 16:h * 16 + 8], on[h * 16 + 8:h * 16 + 16]
        onw[h] = jnp.concatenate([low, low, high, high], axis=1)

    def window(xf, it, h):
        rows16 = pl.ds(h * 16, 16)
        spec = xf[it, :, :, rows16, :].reshape(32, 16, 128).astype(F32)
        both = jnp.concatenate([spec[:, :8].reshape(256, 128), spec[:, 8:].reshape(256, 128)], axis=1)
        lane = lax.rem(lax.broadcasted_iota(jnp.int32, (256, 256), 1), 128)
        real = jnp.where(lane < 64, both, 0.0).astype(BF)
        imag = jnp.where(lane < 64, 0.0, both).astype(BF)
        stacked = jnp.concatenate([real, imag], axis=0)
        traces = jnp.dot(first[...], stacked, preferred_element_type=F32).reshape(64, 8, 256)
        times = lax.broadcasted_iota(jnp.int32, (64, 8, 256), 0)
        kept = jnp.where(times < onw[h][None], traces, 0.0).astype(BF).reshape(512, 256)
        back = jnp.dot(second[fme], kept, preferred_element_type=F32)
        lane = lax.rem(lax.broadcasted_iota(jnp.int32, (64, 256), 1), 128)
        chosen = jnp.where(lane < 64, back[:64], back[64:]).reshape(8, 8, 256)
        return jnp.concatenate([chosen[:, :, :128], chosen[:, :, 128:]], axis=1)

    def gather_freq(xf, it, d, base):
        return copy(xf.at[it, fme], xf.at[it, fme], ssem.at[it, base + d], rsem.at[it, base + d], freq_on(d))

    def recv_freq(xf, it, d, base):
        g = wrap(fme - d)
        return copy(xf.at[it, g], xf.at[it, g], ssem.at[it, base + d], rsem.at[it, base + d], freq_on(d))

    def send_rows(it, d, cp):
        j = wrap(v + d) * 2 + cp
        return copy(s1.at[it, j], r1.at[it, d * 2 + c], ssem.at[it, 8 + d * 2 + cp], rsem.at[it, 8 + d * 2 + c],
                    on_ring(d, cp))

    def partner_rows(it):
        return copy(s1.at[it, v * 2 + 1 - c], r1.at[it, c], ssem.at[it, 8], rsem.at[it, 8 + c], partner)

    def recv_rows(it, d, cs):
        return copy(s1.at[it, 0], r1.at[it, d * 2 + cs], ssem.at[it, 8], rsem.at[it, 8 + d * 2 + cs], partner)

    def send_minus(it, d, cp):
        slot = (x if cp == 0 else y) * 2 + c
        return copy(minus.at[it], mblk.at[it, :, pl.ds(pl.multiple_of(slot * 32, 32), 32), :],
                    ssem.at[it, 20 + d * 2 + cp], rsem.at[it, 20 + d * 2 + c], to_ring(d, cp))

    def partner_minus(it):
        slot = jnp.where(zero, y, x) * 2 + c
        return copy(minus.at[it], mblk.at[it, :, pl.ds(pl.multiple_of(slot * 32, 32), 32), :],
                    ssem.at[it, 20], rsem.at[it, 20 + c], partner)

    def recv_minus(it, d, cs):
        slot = wrap(v - d) * 2 + cs
        return copy(minus.at[it], mblk.at[it, :, pl.ds(pl.multiple_of(slot * 32, 32), 32), :],
                    ssem.at[it, 20], rsem.at[it, 20 + d * 2 + cs], partner)

    def send_sources(it, du, dz):
        k = wrap(u + du) * 2 + lax.rem(z + dz, 2)
        i = du * 2 + dz
        return copy(s2.at[it, k], r2.at[it, i], ssem.at[it, 28 + i], rsem.at[it, 28 + i], ring_u(du, dz))

    def total(r, it, keep):
        def step(f, carry):
            acc = r[it, 0, f].astype(F32)
            for i in range(1, 8):
                acc = acc + r[it, i, f].astype(F32)
            keep[it, fme, f] = acc.astype(BF)
            return carry
        lax.fori_loop(0, 8, step, 0)

    ring = [(d, cp) for d in (2, 1, 3) for cp in range(2)]

    def iteration(it, carry):
        @pl.when(it > 0)
        def _():
            for du, dz in around:
                gather_plus(it, du, dz).start()
        own = u * 2 + z
        pblk[it, :, pl.ds(pl.multiple_of(own * 32, 32), 32), :] = plus[it]
        for du, dz in around:
            recv_plus(it, du, dz).wait_recv()

        @pl.when(it == 0)
        def _():
            for d, cs in ring:
                recv_reflection(d, cs).wait_recv()
            recv_reflection(0, 1 - c).wait_recv()

        def forward(f, carry):
            block = pblk[it, f]
            out = jnp.dot(rblk[f, 0], block, preferred_element_type=F32)
            out = out + jnp.dot(rblk[f, 1], turned(block, 1), preferred_element_type=F32)
            s1[it, :, f] = out.astype(BF).reshape(8, 32, 128)
            return carry
        lax.fori_loop(0, 8, forward, 0)
        for d, cp in ring:
            send_rows(it, d, cp).start()
        partner_rows(it).start()
        r1[it, c] = s1[it, mine]

        @pl.when(it == 0)
        def _():
            def flip(f, carry):
                for part in range(2):
                    rtrans[f, part] = rblk[f, part].T
                return carry
            lax.fori_loop(0, 8, flip, 0)

        for d, cs in ring:
            recv_rows(it, d, cs).wait_recv()
        recv_rows(it, 0, 1 - c).wait_recv()
        total(r1, it, xf1)
        for d in (2, 1, 3):
            gather_freq(xf1, it, d, 16).start()
        for d in (1, 3, 2):
            recv_freq(xf1, it, d, 16).wait_recv()
        for h in range(2):
            value = window(xf1, it, h).astype(BF)
            minus[it, :, pl.ds(h * 16, 16), :] = value
            minus_out[:, pl.ds(h * 16, 16), :] = value

        for d, cp in ring:
            send_minus(it, d, cp).start()
        partner_minus(it).start()
        mblk[it, :, pl.ds(pl.multiple_of(mine * 32, 32), 32), :] = minus[it]
        for d, cs in ring:
            recv_minus(it, d, cs).wait_recv()
        recv_minus(it, 0, 1 - c).wait_recv()

        def adjoint(f, carry):
            block = mblk[it, f]
            out = jnp.dot(rtrans[f, 0], block, preferred_element_type=F32)
            out = out + jnp.dot(rtrans[f, 1], turned(block, -1), preferred_element_type=F32)
            s2[it, :, f] = out.astype(BF).reshape(8, 32, 128)
            return carry
        lax.fori_loop(0, 8, adjoint, 0)
        for du, dz in around:
            send_sources(it, du, dz).start()
        r2[it, 0] = s2[it, own]
        for du, dz in around:
            send_sources(it, du, dz).wait_recv()
        total(r2, it, xf2)
        for d in (2, 1, 3):
            gather_freq(xf2, it, d, 36).start()
        for d in (1, 3, 2):
            recv_freq(xf2, it, d, 36).wait_recv()
        for h in range(2):
            rows16 = pl.ds(h * 16, 16)
            value = (direct[:, rows16, :].astype(F32) + window(xf2, it, h)).astype(BF)
            plus[it + 1, :, rows16, :] = value
            plus_out[:, rows16, :] = value

        for du, dz in around:
            gather_plus(it, du, dz).wait_send()
            send_sources(it, du, dz).wait_send()
        for d, cp in ring:
            send_rows(it, d, cp).wait_send()
            send_minus(it, d, cp).wait_send()
        partner_rows(it).wait_send()
        partner_minus(it).wait_send()
        for d in (1, 2, 3):
            gather_freq(xf1, it, d, 16).wait_send()
            gather_freq(xf2, it, d, 36).wait_send()
        return carry

    lax.fori_loop(0, ITERS, iteration, 0)
    for d, cp in ring:
        send_reflection(d, cp).wait_send()
    partner_reflection().wait_send()


def local(reflection, focus_direct, onsets):
    first, second = window_tables()
    block = jax.ShapeDtypeStruct((8, 32, 128), BF)
    vmem = pl.BlockSpec(memory_space=pltpu.VMEM)
    return pl.pallas_call(
        kernel,
        out_shape=(block, block),
        in_specs=[vmem] * 5,
        out_specs=(vmem, vmem),
        scratch_shapes=[
            pltpu.VMEM((8, 8, 2, 32, 256), BF),
            pltpu.VMEM((8, 2, 256, 256), BF),
            pltpu.VMEM((8, 2, 256, 256), BF),
            pltpu.VMEM((ITERS + 1, 8, 32, 128), BF),
            pltpu.VMEM((ITERS, 8, 256, 128), BF),
            pltpu.VMEM((ITERS, 8, 8, 32, 128), BF),
            pltpu.VMEM((ITERS, 8, 8, 32, 128), BF),
            pltpu.VMEM((ITERS, 4, 8, 32, 128), BF),
            pltpu.VMEM((ITERS, 8, 32, 128), BF),
            pltpu.VMEM((ITERS, 8, 256, 128), BF),
            pltpu.VMEM((ITERS, 8, 8, 32, 128), BF),
            pltpu.VMEM((ITERS, 8, 8, 32, 128), BF),
            pltpu.VMEM((ITERS, 4, 8, 32, 128), BF),
            pltpu.VMEM((2, 8, 256), jnp.int32),
            pltpu.SemaphoreType.DMA((8,)),
            pltpu.SemaphoreType.DMA((8,)),
            pltpu.SemaphoreType.DMA((ITERS, 40)),
            pltpu.SemaphoreType.DMA((ITERS, 40)),
        ],
        compiler_params=pltpu.CompilerParams(
            collective_id=0, has_side_effects=True, vmem_limit_bytes=48 * 1024 * 1024),
        name="marchenko",
    )(reflection, focus_direct, onsets, jnp.asarray(first), jnp.asarray(second))


def solution(mesh):
    in_specs = (P("freq", None, "rows", None), P("freq", "rows", None), P("rows", None))
    out_specs = (P("freq", "rows", None), P("freq", "rows", None))
    return jax.shard_map(local, mesh=mesh, in_specs=in_specs, out_specs=out_specs, check_vma=False)
```

time: 1190 us -> 129 us (0.11)
  waiting for transfers between devices: 823 us -> 0 us
  blocking collectives: 234 us -> 0 us
  Pallas kernels: 0 us -> 121 us
  local copies, waits for them, and re-layouts: 51.4 us -> 6.48 us
  matrix products: 26 us -> 0 us
  other arithmetic: 22.2 us -> 0 us
  between operations: 14.1 us -> 0.65 us
  starting transfers between devices: 12.6 us -> 0 us
    reduce_scatter x2 -> x0, waiting for transfers between devices: 588 us -> none  [local(): lax.psum_scatter(moved, 'rows', scatter_dimension=1, tiled=True)]
    all_to_all x6 -> x0, blocking collectives: 234 us -> none  [the longest x2 190 us: local(): lax.all_to_all(blocks.astype(jnp.bfloat16), 'freq', split_axis=2, concat_...]
    all_gather x2 -> x0, waiting for transfers between devices: 220 us -> none  [local(): gathered = lax.all_gather(plus, 'rows', axis=1, tiled=True)]
    pallas_call x0 -> x1, Pallas kernels: none -> 121 us  [local(): pl.pallas_call(kernel, out_shape=(block, block), in_specs=[vmem] * 5, out...]
    dot_general x20 -> x0, matrix products: 26 us -> none  [the longest x2 6.04 us: local(): jnp.einsum('fcrs,fsq->fcrq', reflection, gathered, preferred_element_type...]
    convert_element_type x4 -> x0, local copies, waits for them, and re-layouts: 22.9 us -> none  [the longest x2 16.2 us: local(): moved = lax.all_to_all(blocks.astype(jnp.bfloat16), 'freq', split_axis=2,...]
    concatenate x8 -> x0, local copies, waits for them, and re-layouts: 14.5 us -> none  [the longest x2 13.1 us: adjoint_combine(): return jnp.concatenate([real_out, imag_out], axis=-1)]
    another operation x4 -> x0, other arithmetic: 13.3 us -> none
  transfers between devices with their start and end apart: 6 -> 0, of which waited for: 6 -> 0; matrix products, arithmetic and copies ran while one was open for 0% -> 0% of each run, Pallas kernels for 0% -> 0%
where the time goes in v1:
time: 129 us
  Pallas kernels  121 us (94%)
  local copies, waits for them, and re-layouts  6.48 us (5%)
    pallas_call x1, Pallas kernels, local(): pl.pallas_call(kernel, out_shape=(block, block), in_specs=[vmem] * 5, out...  121 us
    unnamed x12, local copies, waits for them, and re-layouts  6.48 us

profile of v1, /device:TPU:1, one launch (start us, length us, event | category | flops | bytes accessed | tf_op | source)
XLA Modules:
  0.0 128.6 jit_solution(6399182518070276135)
XLA Ops:
  0.6 0.0 copy-start
  0.6 1.6 %copy-done = bf16[8,2,32,2048]{3,2,1,0:T(8,128)(2,1)S(1)} copy-done((bf16[8,2,32,2048]{3,2,1,0:T(8,128)(2,1)S(1)}, bf16[8,2,32,2048]{3,2,1,0:T(8,128)(2,1)}, u32[]{:S(2)}) %copy-start) | copy-done | bytes 2097176
  2.2 0.0 copy-start.1
  2.2 1.0 copy-done.1
  3.3 0.0 copy-start.2
  3.3 1.0 copy-done.2
  4.3 0.0 copy-start.3
  4.3 0.8 copy-done.3
  5.1 0.0 copy-start.4
  5.1 0.7 copy-done.4
  5.9 121.5 %marchenko.1 = (bf16[8,32,128]{2,1,0:T(8,128)(2,1)S(1)}, bf16[8,32,128]{2,1,0:T(8,128)(2,1)S(1)}) custom-call(bf16[8,2,32,2048]{3,2,1,0:T(8,128)(2,1)S(1)} %copy-done, bf16[8,32,128]{2,1,0:T(8,128)(2,1)S(1)} %copy-done.3, s32[32,64]{1,0:T(8,128)S(1)} %copy-done.4, bf16[512,512]{1,0:T(8,128)(2,1)S(1)} %copy-done.2, bf16[4,128,512]{2,1,0:T(8,128)(2,1)S(1)} %copy-done.1), custom_call_target="tpu_custom_call" | custom-call | tf_op jit(solution)/shard_map/marchenko/pallas_call | solution.py:321
  127.3 0.6 copy.9
  128.0 0.6 copy.10
Async XLA Ops:
  0.6 1.6 %copy-start = (bf16[8,2,32,2048]{3,2,1,0:T(8,128)(2,1)S(1)}, bf16[8,2,32,2048]{3,2,1,0:T(8,128)(2,1)}, u32[]{:S(2)}) copy-start(bf16[8,2,32,2048]{3,2,1,0:T(8,128)(2,1)} %refl.1) | copy-start | bytes 6291460
  2.2 1.0 copy-start.1
  3.3 1.0 copy-start.2
  4.3 0.8 copy-start.3
  5.1 0.7 copy-start.4

commit v2 on v0

v2 whole, which is shorter than its diff:
```python
import math

import jax
import jax.numpy as jnp
import numpy as np
from jax import lax
from jax.experimental import pallas as pl
from jax.experimental.pallas import tpu as pltpu
from jax.sharding import PartitionSpec as P

NT = 128
ITERS = 2
MESH = pl.DeviceIdType.MESH
BF = jnp.bfloat16
F32 = jnp.float32
Q = 2
F = 8 // Q


def window_tables():
    t = np.arange(64)[:, None]
    k = np.arange(1, 33)[None, :]
    ang = 2.0 * np.pi * ((t * k) % NT) / NT
    parts = np.stack([np.cos(ang), np.sin(ang)])
    eye = np.eye(8)
    first = np.einsum("ctf,rs->trcfs", parts, eye).reshape(512, 512)
    weight = np.where(np.arange(64) == 0, 2.0, 4.0) / NT
    back = parts * weight[None, :, None]
    second = np.einsum("ctgqf,rs->gqcfrts", back.reshape(2, 64, 4, Q, F), eye).reshape(4, 128, 512)
    return first.astype(jnp.bfloat16), second.astype(jnp.bfloat16)


def turned(block, sign):
    real, imag = block[:, :64], block[:, 64:]
    if sign > 0:
        return jnp.concatenate([-imag, real], axis=1)
    return jnp.concatenate([imag, -real], axis=1)


def kernel(refl_hbm, direct_hbm, onsets_hbm, first_hbm, second_hbm, plus_out, minus_out,
           refl, direct, onsets, first, second,
           rsend, rblk, rtrans, plus, pblk, s1, r1, xf1, minus, mblk, s2, r2, xf2, kept, onw,
           lsem, rsnd, rrcv, ssem, rsem):
    fme = lax.axis_index("freq")
    row = lax.axis_index("rows")
    c = lax.rem(row, 2)
    x = lax.rem(row // 2, 4)
    z = lax.rem(row // 8, 2)
    y = row // 16
    zero = c == 0
    u = jnp.where(zero, y, x)
    v = jnp.where(zero, x, y)

    def rows(y, z, x, c):
        return ((y * 2 + z) * 4 + x) * 2 + c

    def wrap(a):
        return lax.rem(a + 8, 4)

    def ring_u(du, dz):
        up, zp = wrap(u + du), lax.rem(z + dz, 2)
        return (fme, jnp.where(zero, rows(up, zp, x, c), rows(y, zp, up, c)))

    def to_ring(d, cp):
        return (fme, rows(y, z, wrap(x + d), 0) if cp == 0 else rows(wrap(y + d), z, x, 1))

    def on_ring(d, cp):
        vp = wrap(v + d)
        return (fme, jnp.where(zero, rows(y, z, vp, cp), rows(vp, z, x, cp)))

    partner = (fme, rows(y, z, x, 1 - c))

    def freq_on(d):
        return (wrap(fme + d), row)

    around = [(du, dz) for du in (2, 1, 3, 0) for dz in (1, 0) if (du, dz) != (0, 0)]
    ring = [(d, cp) for d in (2, 1, 3) for cp in range(2)]

    bar = pltpu.get_barrier_semaphore()
    peers = [partner]
    peers += [ring_u(du, dz) for du, dz in around]
    peers += [to_ring(d, cp) for d, cp in ring]
    peers += [on_ring(d, cp) for d, cp in ring]
    peers += [freq_on(d) for d in range(1, 4)]
    for q in peers:
        pl.semaphore_signal(bar, inc=1, device_id=q, device_id_type=MESH)
    loads = [pltpu.make_async_copy(refl_hbm, refl, lsem.at[0]), pltpu.make_async_copy(direct_hbm, direct, lsem.at[1]),
             pltpu.make_async_copy(onsets_hbm, onsets, lsem.at[2]), pltpu.make_async_copy(first_hbm, first, lsem.at[3]),
             pltpu.make_async_copy(second_hbm.at[fme], second, lsem.at[4])]
    for load in loads:
        load.start()

    def copy(src, dst, send, recv, device):
        return pltpu.make_async_remote_copy(
            src_ref=src, dst_ref=dst, send_sem=send, recv_sem=recv, device_id=device, device_id_type=MESH)

    def pieces(cp, w):
        if cp == 0:
            return [(k * 256 + w * 64) for k in range(8)]
        return [((w * 2 + k % 2) * 256 + (k // 2) * 64 + 32) for k in range(8)]

    def arrange(q):
        def step(i, carry):
            block = refl[q * F + i].reshape(64, 2048)
            for cp in range(2):
                for w in range(4):
                    out = jnp.concatenate([block[:, p:p + 32] for p in pieces(cp, w)], axis=1)
                    rsend[q, cp * 4 + w, i] = out.reshape(2, 32, 256)
            return carry
        lax.fori_loop(0, F, step, 0)

    mine = v * 2 + c
    own = u * 2 + z

    def send_reflection(q, d, cp):
        place = x if cp == 0 else y
        return copy(rsend.at[q, cp * 4 + wrap(place + d)], rblk.at[q, place * 2 + c],
                    rsnd.at[q, d * 2 + cp], rrcv.at[q, d * 2 + c], to_ring(d, cp))

    def partner_reflection(q):
        return copy(rsend.at[q, (1 - c) * 4 + u], rblk.at[q, u * 2 + c], rsnd.at[q, 0], rrcv.at[q, c], partner)

    def recv_reflection(q, d, cs):
        return copy(rsend.at[q, 0], rblk.at[q, wrap(v - d) * 2 + cs], rsnd.at[q, 0], rrcv.at[q, d * 2 + cs], partner)

    def send_plus(it, q, du, dz):
        i = du * 2 + dz
        return copy(plus.at[it, q], pblk.at[it, q, own], ssem.at[it, q, i], rsem.at[it, q, i], ring_u(du, dz))

    def recv_plus(it, q, du, dz):
        slot = wrap(u - du) * 2 + lax.rem(z + dz, 2)
        i = du * 2 + dz
        return copy(plus.at[it, q], pblk.at[it, q, slot], ssem.at[it, q, i], rsem.at[it, q, i], ring_u(du, dz))

    def send_rows(it, q, d, cp):
        return copy(s1.at[it, q, wrap(v + d) * 2 + cp], r1.at[it, q, d * 2 + c],
                    ssem.at[it, q, 8 + d * 2 + cp], rsem.at[it, q, 8 + d * 2 + c], on_ring(d, cp))

    def partner_rows(it, q):
        return copy(s1.at[it, q, v * 2 + 1 - c], r1.at[it, q, c], ssem.at[it, q, 8], rsem.at[it, q, 8 + c], partner)

    def recv_rows(it, q, d, cs):
        return copy(s1.at[it, q, 0], r1.at[it, q, d * 2 + cs], ssem.at[it, q, 8], rsem.at[it, q, 8 + d * 2 + cs], partner)

    def send_freq(xf, it, q, d, base):
        return copy(xf.at[it, q, fme], xf.at[it, q, fme], ssem.at[it, q, base + d], rsem.at[it, q, base + d], freq_on(d))

    def recv_freq(xf, it, q, d, base):
        g = wrap(fme - d)
        return copy(xf.at[it, q, g], xf.at[it, q, g], ssem.at[it, q, base + d], rsem.at[it, q, base + d], freq_on(d))

    def send_minus(it, q, d, cp):
        place = x if cp == 0 else y
        return copy(minus.at[it, q], mblk.at[it, q, place * 2 + c],
                    ssem.at[it, q, 20 + d * 2 + cp], rsem.at[it, q, 20 + d * 2 + c], to_ring(d, cp))

    def partner_minus(it, q):
        return copy(minus.at[it, q], mblk.at[it, q, u * 2 + c], ssem.at[it, q, 20], rsem.at[it, q, 20 + c], partner)

    def recv_minus(it, q, d, cs):
        return copy(minus.at[it, q], mblk.at[it, q, wrap(v - d) * 2 + cs],
                    ssem.at[it, q, 20], rsem.at[it, q, 20 + d * 2 + cs], partner)

    def send_sources(it, q, du, dz):
        i = du * 2 + dz
        return copy(s2.at[it, q, wrap(u + du) * 2 + lax.rem(z + dz, 2)], r2.at[it, q, i],
                    ssem.at[it, q, 28 + i], rsem.at[it, q, 28 + i], ring_u(du, dz))

    loads[1].wait()
    for q in range(Q):
        plus[0, q] = direct[q * F:(q + 1) * F]
    loads[0].wait()
    for q in range(Q):
        arrange(q)
        if q == 0:
            pl.semaphore_wait(bar, len(peers))
        for d, cp in ring:
            send_reflection(q, d, cp).start()
        partner_reflection(q).start()
        for du, dz in around:
            send_plus(0, q, du, dz).start()
        rblk[q, mine] = rsend[q, c * 4 + v]

    loads[2].wait()
    on = onsets[...]
    for h in range(2):
        low, high = on[h * 16:h * 16 + 8], on[h * 16 + 8:h * 16 + 16]
        onw[h] = jnp.concatenate([low, low, high, high], axis=1)
    loads[3].wait()
    loads[4].wait()

    def window_in(xf, it):
        for h in range(2):
            spec = [xf[it, q, g, :, h * 16:(h + 1) * 16, :] for g in range(4) for q in range(Q)]
            spec = jnp.concatenate(spec, axis=0).astype(F32)
            both = jnp.concatenate([spec[:, :8].reshape(256, 128), spec[:, 8:].reshape(256, 128)], axis=1)
            lane = lax.rem(lax.broadcasted_iota(jnp.int32, (256, 256), 1), 128)
            real = jnp.where(lane < 64, both, 0.0).astype(BF)
            imag = jnp.where(lane < 64, 0.0, both).astype(BF)
            stacked = jnp.concatenate([real, imag], axis=0)
            traces = jnp.dot(first[...], stacked, preferred_element_type=F32).reshape(64, 8, 256)
            times = lax.broadcasted_iota(jnp.int32, (64, 8, 256), 0)
            kept[h] = jnp.where(times < onw[h][None], traces, 0.0).astype(BF).reshape(512, 256)

    def window_out(q, h):
        back = jnp.dot(second[q * 16 * F:(q + 1) * 16 * F], kept[h], preferred_element_type=F32)
        lane = lax.rem(lax.broadcasted_iota(jnp.int32, (8 * F, 256), 1), 128)
        chosen = jnp.where(lane < 64, back[:8 * F], back[8 * F:]).reshape(F, 8, 256)
        return jnp.concatenate([chosen[:, :, :128], chosen[:, :, 128:]], axis=1)

    def total(r, it, q, keep):
        def step(f, carry):
            acc = r[it, q, 0, f].astype(F32)
            for i in range(1, 8):
                acc = acc + r[it, q, i, f].astype(F32)
            keep[it, q, fme, f] = acc.astype(BF)
            return carry
        lax.fori_loop(0, F, step, 0, unroll=True)

    def iteration(it, carry):
        for q in range(Q):
            pblk[it, q, own] = plus[it, q]
        for q in range(Q):
            for du, dz in around:
                recv_plus(it, q, du, dz).wait_recv()

            @pl.when(it == 0)
            def _():
                for d, cs in ring:
                    recv_reflection(q, d, cs).wait_recv()
                recv_reflection(q, 0, 1 - c).wait_recv()

            def forward(i, carry):
                block = pblk[it, q, :, i].reshape(256, 128)
                out = jnp.dot(rblk[q, :, i, 0].reshape(256, 256), block, preferred_element_type=F32)
                out = out + jnp.dot(rblk[q, :, i, 1].reshape(256, 256), turned(block, 1), preferred_element_type=F32)
                s1[it, q, :, i] = out.astype(BF).reshape(8, 32, 128)
                return carry
            lax.fori_loop(0, F, forward, 0, unroll=True)
            for d, cp in ring:
                send_rows(it, q, d, cp).start()
            partner_rows(it, q).start()
            r1[it, q, c] = s1[it, q, mine]

        @pl.when(it == 0)
        def _():
            for q in range(Q):
                def flip(i, carry):
                    for part in range(2):
                        rtrans[q * F + i, part] = rblk[q, :, i, part].reshape(256, 256).T
                    return carry
                lax.fori_loop(0, F, flip, 0)

        for q in range(Q):
            for d, cs in ring:
                recv_rows(it, q, d, cs).wait_recv()
            recv_rows(it, q, 0, 1 - c).wait_recv()
            total(r1, it, q, xf1)
            for d in (2, 1, 3):
                send_freq(xf1, it, q, d, 16).start()
        for q in range(Q):
            for d in (1, 3, 2):
                recv_freq(xf1, it, q, d, 16).wait_recv()
        window_in(xf1, it)

        for q in range(Q):
            for h in range(2):
                value = window_out(q, h).astype(BF)
                minus[it, q, :, h * 16:(h + 1) * 16, :] = value
                minus_out[q * F:(q + 1) * F, h * 16:(h + 1) * 16, :] = value
            for d, cp in ring:
                send_minus(it, q, d, cp).start()
            partner_minus(it, q).start()
            mblk[it, q, mine] = minus[it, q]
        for q in range(Q):
            for d, cs in ring:
                recv_minus(it, q, d, cs).wait_recv()
            recv_minus(it, q, 0, 1 - c).wait_recv()

            def adjoint(i, carry):
                block = mblk[it, q, :, i].reshape(256, 128)
                out = jnp.dot(rtrans[q * F + i, 0], block, preferred_element_type=F32)
                out = out + jnp.dot(rtrans[q * F + i, 1], turned(block, -1), preferred_element_type=F32)
                s2[it, q, :, i] = out.astype(BF).reshape(8, 32, 128)
                return carry
            lax.fori_loop(0, F, adjoint, 0, unroll=True)
            for du, dz in around:
                send_sources(it, q, du, dz).start()
            r2[it, q, 0] = s2[it, q, own]
        for q in range(Q):
            for du, dz in around:
                send_sources(it, q, du, dz).wait_recv()
            total(r2, it, q, xf2)
            for d in (2, 1, 3):
                send_freq(xf2, it, q, d, 36).start()
        for q in range(Q):
            for d in (1, 3, 2):
                recv_freq(xf2, it, q, d, 36).wait_recv()
        window_in(xf2, it)
        for q in range(Q):
            for h in range(2):
                rows16 = slice(h * 16, (h + 1) * 16)
                value = (direct[q * F:(q + 1) * F, rows16, :].astype(F32) + window_out(q, h)).astype(BF)
                plus[it + 1, q, :, rows16, :] = value
                plus_out[q * F:(q + 1) * F, rows16, :] = value

            @pl.when(it + 1 < ITERS)
            def _():
                for du, dz in around:
                    send_plus(it + 1, q, du, dz).start()

        for q in range(Q):
            for du, dz in around:
                send_plus(it, q, du, dz).wait_send()
                send_sources(it, q, du, dz).wait_send()
            for d, cp in ring:
                send_rows(it, q, d, cp).wait_send()
                send_minus(it, q, d, cp).wait_send()
            partner_rows(it, q).wait_send()
            partner_minus(it, q).wait_send()
            for d in (1, 2, 3):
                send_freq(xf1, it, q, d, 16).wait_send()
                send_freq(xf2, it, q, d, 36).wait_send()
        return carry

    lax.fori_loop(0, ITERS, iteration, 0)
    for q in range(Q):
        for d, cp in ring:
            send_reflection(q, d, cp).wait_send()
        partner_reflection(q).wait_send()


def local(reflection, focus_direct, onsets):
    first, second = window_tables()
    block = jax.ShapeDtypeStruct((8, 32, 128), BF)
    vmem = pl.BlockSpec(memory_space=pltpu.VMEM)
    part = (F, 32, 128)
    return pl.pallas_call(
        kernel,
        out_shape=(block, block),
        in_specs=[pl.BlockSpec(memory_space=pl.ANY)] * 5,
        out_specs=(vmem, vmem),
        scratch_shapes=[
            pltpu.VMEM((8, 2, 32, 2048), BF),
            pltpu.VMEM((8, 32, 128), BF),
            pltpu.VMEM((32, 64), jnp.int32),
            pltpu.VMEM((512, 512), BF),
            pltpu.VMEM((128, 512), BF),
            pltpu.VMEM((Q, 8, F, 2, 32, 256), BF),
            pltpu.VMEM((Q, 8, F, 2, 32, 256), BF),
            pltpu.VMEM((8, 2, 256, 256), BF),
            pltpu.VMEM((ITERS + 1, Q) + part, BF),
            pltpu.VMEM((ITERS, Q, 8) + part, BF),
            pltpu.VMEM((ITERS, Q, 8) + part, BF),
            pltpu.VMEM((ITERS, Q, 8) + part, BF),
            pltpu.VMEM((ITERS, Q, 4) + part, BF),
            pltpu.VMEM((ITERS, Q) + part, BF),
            pltpu.VMEM((ITERS, Q, 8) + part, BF),
            pltpu.VMEM((ITERS, Q, 8) + part, BF),
            pltpu.VMEM((ITERS, Q, 8) + part, BF),
            pltpu.VMEM((ITERS, Q, 4) + part, BF),
            pltpu.VMEM((2, 512, 256), BF),
            pltpu.VMEM((2, 8, 256), jnp.int32),
            pltpu.SemaphoreType.DMA((5,)),
            pltpu.SemaphoreType.DMA((Q, 8)),
            pltpu.SemaphoreType.DMA((Q, 8)),
            pltpu.SemaphoreType.DMA((ITERS, Q, 40)),
            pltpu.SemaphoreType.DMA((ITERS, Q, 40)),
        ],
        compiler_params=pltpu.CompilerParams(
            collective_id=0, has_side_effects=True, vmem_limit_bytes=60 * 1024 * 1024),
        name="marchenko",
    )(reflection, focus_direct, onsets, jnp.asarray(first), jnp.asarray(second))


def solution(mesh):
    in_specs = (P("freq", None, "rows", None), P("freq", "rows", None), P("rows", None))
    out_specs = (P("freq", "rows", None), P("freq", "rows", None))
    return jax.shard_map(local, mesh=mesh, in_specs=in_specs, out_specs=out_specs, check_vma=False)
```

time: 1190 us -> 105 us (0.09)
  waiting for transfers between devices: 823 us -> 0 us
  blocking collectives: 234 us -> 0 us
  Pallas kernels: 0 us -> 102 us
  local copies, waits for them, and re-layouts: 51.4 us -> 2.95 us
  matrix products: 26 us -> 0 us
  other arithmetic: 22.2 us -> 0 us
  between operations: 14.1 us -> 0.64 us
  starting transfers between devices: 12.6 us -> 0 us
    reduce_scatter x2 -> x0, waiting for transfers between devices: 588 us -> none  [local(): lax.psum_scatter(moved, 'rows', scatter_dimension=1, tiled=True)]
    all_to_all x6 -> x0, blocking collectives: 234 us -> none  [the longest x2 190 us: local(): lax.all_to_all(blocks.astype(jnp.bfloat16), 'freq', split_axis=2, concat_...]
    all_gather x2 -> x0, waiting for transfers between devices: 220 us -> none  [local(): gathered = lax.all_gather(plus, 'rows', axis=1, tiled=True)]
    pallas_call x0 -> x1, Pallas kernels: none -> 102 us  [local(): pl.pallas_call(kernel, out_shape=(block, block), in_specs=[pl.BlockSpec(m...]
    dot_general x20 -> x0, matrix products: 26 us -> none  [the longest x2 6.04 us: local(): jnp.einsum('fcrs,fsq->fcrq', reflection, gathered, preferred_element_type...]
    convert_element_type x4 -> x0, local copies, waits for them, and re-layouts: 22.9 us -> none  [the longest x2 16.2 us: local(): moved = lax.all_to_all(blocks.astype(jnp.bfloat16), 'freq', split_axis=2,...]
    concatenate x8 -> x0, local copies, waits for them, and re-layouts: 14.5 us -> none  [the longest x2 13.1 us: adjoint_combine(): return jnp.concatenate([real_out, imag_out], axis=-1)]
    another operation x4 -> x0, other arithmetic: 13.3 us -> none
  transfers between devices with their start and end apart: 6 -> 0, of which waited for: 6 -> 0; matrix products, arithmetic and copies ran while one was open for 0% -> 0% of each run, Pallas kernels for 0% -> 0%
where the time goes in v2:
time: 105 us
  Pallas kernels  102 us (97%)
  local copies, waits for them, and re-layouts  2.95 us (3%)
    pallas_call x1, Pallas kernels, local(): pl.pallas_call(kernel, out_shape=(block, block), in_specs=[pl.BlockSpec(m...  102 us
    unnamed x2, local copies, waits for them, and re-layouts  2.95 us

profile of v2, /device:TPU:1, one launch (start us, length us, event | category | flops | bytes accessed | tf_op | source)
XLA Modules:
  0.0 105.2 jit_solution(15579016076816960994)
XLA Ops:
  0.6 101.7 %marchenko.1 = (bf16[8,32,128]{2,1,0:T(8,128)(2,1)}, bf16[8,32,128]{2,1,0:T(8,128)(2,1)}) custom-call(bf16[8,2,32,2048]{3,2,1,0:T(8,128)(2,1)} %refl_hbm.1, bf16[8,32,128]{2,1,0:T(8,128)(2,1)} %direct_hbm.1, s32[32,64]{1,0:T(8,128)} %onsets_hbm.1, bf16[512,512]{1,0:T(8,128)(2,1)} %constant.4.clone.first_hbm, bf16[4,128,512]{2,1,0:T(8,128)(2,1)} %constant.5.clone.second_hbm), custom_call_target="tpu_custom_call" | custom-call | tf_op jit(solution)/shard_map/marchenko/pallas_call | solution.py:338
  102.3 1.5 %copy.9 = bf16[8,32,128]{2,1,0:T(8,128)(2,1)} copy(bf16[8,32,128]{2,1,0:T(8,128)(2,1)} %get-tuple-element.4) | data formatting | bytes 131072
  103.8 1.5 %copy.10 = bf16[8,32,128]{2,1,0:T(8,128)(2,1)} copy(bf16[8,32,128]{2,1,0:T(8,128)(2,1)} %get-tuple-element.5) | data formatting | bytes 131072

commit v3 on v2

v3 whole, which is shorter than its diff:
```python
import math

import jax
import jax.numpy as jnp
import numpy as np
from jax import lax
from jax.experimental import pallas as pl
from jax.experimental.pallas import tpu as pltpu
from jax.sharding import PartitionSpec as P

NT = 128
ITERS = 2
MESH = pl.DeviceIdType.MESH
BF = jnp.bfloat16
F32 = jnp.float32
Q = 2
CHAINS = 2
S = CHAINS * Q
R4 = 4 // Q
F = 8 // Q


def window_tables():
    t = np.arange(64)[:, None]
    k = np.arange(1, 33)[None, :]
    ang = 2.0 * np.pi * ((t * k) % NT) / NT
    parts = np.stack([np.cos(ang), np.sin(ang)])
    eye = np.eye(8)
    paired = parts.reshape(2, 64, 4, Q, R4, 2)
    first = np.einsum("ctgqfo,rs->trcoqgfs", paired, eye).reshape(512, 512)
    weight = np.where(np.arange(64) == 0, 2.0, 4.0) / NT
    back = paired * weight[None, :, None, None, None, None]
    second = np.einsum("ctgqfo,rs->gcoqfrts", back, eye).reshape(4, 128, 512)
    return first.astype(jnp.bfloat16), second.astype(jnp.bfloat16)


def turned(block, sign):
    p = [block[:, 32 * i:32 * i + 32] for i in range(4)]
    if sign > 0:
        return jnp.concatenate([-p[1], p[0], -p[3], p[2]], axis=1)
    return jnp.concatenate([p[1], -p[0], p[3], -p[2]], axis=1)


def kernel(refl_hbm, direct_hbm, onsets_hbm, first_hbm, second_hbm, plus_out, minus_out,
           refl, direct, onsets, first, second,
           rsend, rblk, rtrans, plus, pblk, s1, r1, xf1, minus, mblk, s2, r2, xf2, kept, onw, packed,
           lsem, rsnd, rrcv, ssem, rsem):
    fme = lax.axis_index("freq")
    row = lax.axis_index("rows")
    c = lax.rem(row, 2)
    x = lax.rem(row // 2, 4)
    z = lax.rem(row // 8, 2)
    y = row // 16
    zero = c == 0
    u = jnp.where(zero, y, x)
    v = jnp.where(zero, x, y)

    def rows(y, z, x, c):
        return ((y * 2 + z) * 4 + x) * 2 + c

    def wrap(a):
        return lax.rem(a + 8, 4)

    def ring_u(du, dz):
        up, zp = wrap(u + du), lax.rem(z + dz, 2)
        return (fme, jnp.where(zero, rows(up, zp, x, c), rows(y, zp, up, c)))

    def to_ring(d, cp):
        return (fme, rows(y, z, wrap(x + d), 0) if cp == 0 else rows(wrap(y + d), z, x, 1))

    def on_ring(d, cp):
        vp = wrap(v + d)
        return (fme, jnp.where(zero, rows(y, z, vp, cp), rows(vp, z, x, cp)))

    partner = (fme, rows(y, z, x, 1 - c))

    def freq_on(d):
        return (wrap(fme + d), row)

    around = [(du, dz) for du in (2, 1, 3, 0) for dz in (1, 0) if (du, dz) != (0, 0)]
    ring = [(d, cp) for d in (2, 1, 3) for cp in range(2)]

    bar = pltpu.get_barrier_semaphore()
    peers = [partner]
    peers += [ring_u(du, dz) for du, dz in around]
    peers += [to_ring(d, cp) for d, cp in ring]
    peers += [on_ring(d, cp) for d, cp in ring]
    peers += [freq_on(d) for d in range(1, 4)]
    for q in peers:
        pl.semaphore_signal(bar, inc=1, device_id=q, device_id_type=MESH)
    loads = [pltpu.make_async_copy(refl_hbm, refl, lsem.at[0]), pltpu.make_async_copy(direct_hbm, direct, lsem.at[1]),
             pltpu.make_async_copy(onsets_hbm, onsets, lsem.at[2]), pltpu.make_async_copy(first_hbm, first, lsem.at[3]),
             pltpu.make_async_copy(second_hbm.at[fme], second, lsem.at[4])]
    for load in loads:
        load.start()

    def copy(src, dst, send, recv, device):
        return pltpu.make_async_remote_copy(
            src_ref=src, dst_ref=dst, send_sem=send, recv_sem=recv, device_id=device, device_id_type=MESH)

    def pieces(cp, w):
        if cp == 0:
            return [(k * 256 + w * 64) for k in range(8)]
        return [((w * 2 + k % 2) * 256 + (k // 2) * 64 + 32) for k in range(8)]

    def arrange(q):
        def step(i, carry):
            block = refl[q * F + i].reshape(64, 2048)
            for cp in range(2):
                for w in range(4):
                    out = jnp.concatenate([block[:, p:p + 32] for p in pieces(cp, w)], axis=1)
                    rsend[q, cp * 4 + w, i] = out.reshape(2, 32, 256)
            return carry
        lax.fori_loop(0, F, step, 0)

    mine = v * 2 + c
    own = u * 2 + z

    def send_reflection(q, d, cp):
        place = x if cp == 0 else y
        return copy(rsend.at[q, cp * 4 + wrap(place + d)], rblk.at[q, place * 2 + c],
                    rsnd.at[q], rrcv.at[q], to_ring(d, cp))

    def partner_reflection(q):
        return copy(rsend.at[q, (1 - c) * 4 + u], rblk.at[q, u * 2 + c], rsnd.at[q], rrcv.at[q], partner)

    def wait_for(buffer, count, send, recv):
        return copy(buffer.at[pl.ds(0, count)], buffer.at[pl.ds(0, count)], send, recv, partner)

    def all_reflection(q):
        return wait_for(rblk.at[q], 7, rsnd.at[q], rrcv.at[q])

    def stage(it, q, n):
        return ssem.at[it, q, n], rsem.at[it, q, n]

    def send_plus(it, q, du, dz):
        return copy(plus.at[it, q], pblk.at[it, q, own], *stage(it, q, 0), ring_u(du, dz))

    def all_plus(it, q):
        return wait_for(pblk.at[it, q], 7, *stage(it, q, 0))

    def send_rows(it, q, d, cp):
        return copy(s1.at[it, q, wrap(v + d) * 2 + cp], r1.at[it, q, d * 2 + c], *stage(it, q, 1), on_ring(d, cp))

    def partner_rows(it, q):
        return copy(s1.at[it, q, v * 2 + 1 - c], r1.at[it, q, c], *stage(it, q, 1), partner)

    def all_rows(it, q):
        return wait_for(r1.at[it, q], 7, *stage(it, q, 1))

    def send_freq(xf, it, q, d, n):
        return copy(xf.at[it, q, fme], xf.at[it, q, fme], *stage(it, q, n), freq_on(d))

    def all_freq(xf, it, q, n):
        return wait_for(xf.at[it, q], 3, *stage(it, q, n))

    def send_minus(it, q, d, cp):
        place = x if cp == 0 else y
        return copy(minus.at[it, q], mblk.at[it, q, place * 2 + c], *stage(it, q, 3), to_ring(d, cp))

    def partner_minus(it, q):
        return copy(minus.at[it, q], mblk.at[it, q, u * 2 + c], *stage(it, q, 3), partner)

    def all_minus(it, q):
        return wait_for(mblk.at[it, q], 7, *stage(it, q, 3))

    def send_sources(it, q, du, dz):
        i = du * 2 + dz
        return copy(s2.at[it, q, wrap(u + du) * 2 + lax.rem(z + dz, 2)], r2.at[it, q, i], *stage(it, q, 4), ring_u(du, dz))

    def all_sources(it, q):
        return wait_for(r2.at[it, q], 7, *stage(it, q, 4))

    loads[1].wait()
    for s in range(S):
        h, q = s // Q, s % Q
        for i in range(R4):
            pair = [direct[q * F + 2 * i + o] for o in range(2)]
            value = jnp.concatenate([pair[o][:, e:e + 32] for o in range(2) for e in (32 * h, 64 + 32 * h)], axis=1)
            packed[s, i] = value
            plus[0, s, i] = value
    loads[0].wait()
    for q in range(Q):
        arrange(q)
        if q == 0:
            pl.semaphore_wait(bar, len(peers))
        for d, cp in ring:
            send_reflection(q, d, cp).start()
        partner_reflection(q).start()
        for h in range(CHAINS):
            for du, dz in around:
                send_plus(0, h * Q + q, du, dz).start()
        rblk[q, mine] = rsend[q, c * 4 + v]

    loads[2].wait()
    on = onsets[...]
    for h in range(CHAINS):
        eight = [on[8 * a:8 * a + 8, 32 * h:32 * h + 32] for a in range(4)]
        onw[h] = jnp.concatenate([eight[a] for a in range(4) for _ in range(2)], axis=1)
    loads[3].wait()
    loads[4].wait()

    def window_in(xf, it, h):
        spec = jnp.concatenate([xf[it, h * Q + q].reshape(4 * R4, 32, 128) for q in range(Q)], axis=0).astype(F32)
        odd = [jnp.concatenate([spec[:, 8 * a:8 * a + 8, 64 * o:64 * o + 64] for a in range(4)], axis=2) for o in range(2)]
        both = jnp.concatenate([odd[0].reshape(128, 256), odd[1].reshape(128, 256)], axis=0)
        lane = lax.rem(lax.broadcasted_iota(jnp.int32, (256, 256), 1), 64)
        real = jnp.where(lane < 32, both, 0.0).astype(BF)
        imag = jnp.where(lane < 32, 0.0, both).astype(BF)
        stacked = jnp.concatenate([real, imag], axis=0)
        traces = jnp.dot(first[...], stacked, preferred_element_type=F32).reshape(64, 8, 256)
        times = lax.broadcasted_iota(jnp.int32, (64, 8, 256), 0)
        kept[h] = jnp.where(times < onw[h][None], traces, 0.0).astype(BF).reshape(512, 256)

    def window_out(h):
        back = jnp.dot(second[...], kept[h], preferred_element_type=F32)
        lane = lax.rem(lax.broadcasted_iota(jnp.int32, (64, 256), 1), 64)
        chosen = jnp.where(lane < 32, back[:64], back[64:]).reshape(2, 4, 8, 256)
        return jnp.concatenate(
            [jnp.concatenate([chosen[0, :, :, 64 * a:64 * a + 64], chosen[1, :, :, 64 * a:64 * a + 64]], axis=2)
             for a in range(4)], axis=1)

    def unpack(source, out):
        for q in range(Q):
            for i in range(R4):
                for o in range(2):
                    out[q * F + 2 * i + o] = jnp.concatenate(
                        [source[h * Q + q, i][:, 64 * o + 32 * e:64 * o + 32 * e + 32] for e in range(2) for h in range(CHAINS)],
                        axis=1)

    def total(r, it, q, keep):
        def step(f, carry):
            acc = r[it, q, 0, f].astype(F32)
            for i in range(1, 8):
                acc = acc + r[it, q, i, f].astype(F32)
            keep[it, q, fme, f] = acc.astype(BF)
            return carry
        lax.fori_loop(0, R4, step, 0, unroll=True)

    low = lax.broadcasted_iota(jnp.int32, (256, 128), 1) < 64

    def iteration(it, carry):
        for s in range(S):
            pblk[it, s, own] = plus[it, s]
        for s in range(S):
            q = s % Q
            all_plus(it, s).wait_recv()

            if s < Q:
                @pl.when(it == 0)
                def _():
                    all_reflection(q).wait_recv()

            def forward(i, carry):
                block = pblk[it, s, :, i].reshape(256, 128)
                other = turned(block, 1)
                out = [jnp.dot(rblk[q, :, 2 * i + o, 0].reshape(256, 256), block, preferred_element_type=F32)
                       + jnp.dot(rblk[q, :, 2 * i + o, 1].reshape(256, 256), other, preferred_element_type=F32)
                       for o in range(2)]
                s1[it, s, :, i] = jnp.where(low, out[0], out[1]).astype(BF).reshape(8, 32, 128)
                return carry
            lax.fori_loop(0, R4, forward, 0, unroll=True)
            for d, cp in ring:
                send_rows(it, s, d, cp).start()
            partner_rows(it, s).start()
            r1[it, s, c] = s1[it, s, mine]

        @pl.when(it == 0)
        def _():
            for q in range(Q):
                def flip(i, carry):
                    for part in range(2):
                        rtrans[q * F + i, part] = rblk[q, :, i, part].reshape(256, 256).T
                    return carry
                lax.fori_loop(0, F, flip, 0)

        for s in range(S):
            all_rows(it, s).wait_recv()
            total(r1, it, s, xf1)
            for d in (2, 1, 3):
                send_freq(xf1, it, s, d, 2).start()

        for h in range(CHAINS):
            for s in range(h * Q, h * Q + Q):
                all_freq(xf1, it, s, 2).wait_recv()
            window_in(xf1, it, h)
            value = window_out(h).astype(BF)
            for q in range(Q):
                s = h * Q + q
                minus[it, s] = value[q * R4:(q + 1) * R4]
                for d, cp in ring:
                    send_minus(it, s, d, cp).start()
                partner_minus(it, s).start()
                mblk[it, s, mine] = minus[it, s]
        for s in range(S):
            q = s % Q
            all_minus(it, s).wait_recv()

            def adjoint(i, carry):
                block = mblk[it, s, :, i].reshape(256, 128)
                other = turned(block, -1)
                out = [jnp.dot(rtrans[q * F + 2 * i + o, 0], block, preferred_element_type=F32)
                       + jnp.dot(rtrans[q * F + 2 * i + o, 1], other, preferred_element_type=F32)
                       for o in range(2)]
                s2[it, s, :, i] = jnp.where(low, out[0], out[1]).astype(BF).reshape(8, 32, 128)
                return carry
            lax.fori_loop(0, R4, adjoint, 0, unroll=True)
            for du, dz in around:
                send_sources(it, s, du, dz).start()
            r2[it, s, 0] = s2[it, s, own]
        for s in range(S):
            all_sources(it, s).wait_recv()
            total(r2, it, s, xf2)
            for d in (2, 1, 3):
                send_freq(xf2, it, s, d, 5).start()
        for h in range(CHAINS):
            for s in range(h * Q, h * Q + Q):
                all_freq(xf2, it, s, 5).wait_recv()
            window_in(xf2, it, h)
            value = window_out(h)
            for q in range(Q):
                s = h * Q + q
                plus[it + 1, s] = (packed[s].astype(F32) + value[q * R4:(q + 1) * R4]).astype(BF)

                @pl.when(it + 1 < ITERS)
                def _():
                    for du, dz in around:
                        send_plus(it + 1, s, du, dz).start()

        for s in range(S):
            for copies in (all_plus(it, s), all_rows(it, s), all_freq(xf1, it, s, 2), all_minus(it, s),
                           all_sources(it, s), all_freq(xf2, it, s, 5)):
                copies.wait_send()
        return carry

    lax.fori_loop(0, ITERS, iteration, 0)
    unpack(minus.at[ITERS - 1], minus_out)
    unpack(plus.at[ITERS], plus_out)
    for q in range(Q):
        all_reflection(q).wait_send()


def local(reflection, focus_direct, onsets):
    first, second = window_tables()
    block = jax.ShapeDtypeStruct((8, 32, 128), BF)
    vmem = pl.BlockSpec(memory_space=pltpu.VMEM)
    part = (R4, 32, 128)
    return pl.pallas_call(
        kernel,
        out_shape=(block, block),
        in_specs=[pl.BlockSpec(memory_space=pl.ANY)] * 5,
        out_specs=(vmem, vmem),
        scratch_shapes=[
            pltpu.VMEM((8, 2, 32, 2048), BF),
            pltpu.VMEM((8, 32, 128), BF),
            pltpu.VMEM((32, 64), jnp.int32),
            pltpu.VMEM((512, 512), BF),
            pltpu.VMEM((128, 512), BF),
            pltpu.VMEM((Q, 8, F, 2, 32, 256), BF),
            pltpu.VMEM((Q, 8, F, 2, 32, 256), BF),
            pltpu.VMEM((8, 2, 256, 256), BF),
            pltpu.VMEM((ITERS + 1, S) + part, BF),
            pltpu.VMEM((ITERS, S, 8) + part, BF),
            pltpu.VMEM((ITERS, S, 8) + part, BF),
            pltpu.VMEM((ITERS, S, 8) + part, BF),
            pltpu.VMEM((ITERS, S, 4) + part, BF),
            pltpu.VMEM((ITERS, S) + part, BF),
            pltpu.VMEM((ITERS, S, 8) + part, BF),
            pltpu.VMEM((ITERS, S, 8) + part, BF),
            pltpu.VMEM((ITERS, S, 8) + part, BF),
            pltpu.VMEM((ITERS, S, 4) + part, BF),
            pltpu.VMEM((2, 512, 256), BF),
            pltpu.VMEM((2, 8, 256), jnp.int32),
            pltpu.VMEM((S,) + part, BF),
            pltpu.SemaphoreType.DMA((5,)),
            pltpu.SemaphoreType.DMA((Q,)),
            pltpu.SemaphoreType.DMA((Q,)),
            pltpu.SemaphoreType.DMA((ITERS, S, 6)),
            pltpu.SemaphoreType.DMA((ITERS, S, 6)),
        ],
        compiler_params=pltpu.CompilerParams(
            collective_id=0, has_side_effects=True, vmem_limit_bytes=60 * 1024 * 1024),
        name="marchenko",
    )(reflection, focus_direct, onsets, jnp.asarray(first), jnp.asarray(second))


def solution(mesh):
    in_specs = (P("freq", None, "rows", None), P("freq", "rows", None), P("rows", None))
    out_specs = (P("freq", "rows", None), P("freq", "rows", None))
    return jax.shard_map(local, mesh=mesh, in_specs=in_specs, out_specs=out_specs, check_vma=False)
```

time: 105 us -> 94.8 us (0.903)
  Pallas kernels: 102 us -> 91 us
    pallas_call x1, Pallas kernels: 102 us -> 91 us  [local(): pl.pallas_call(kernel, out_shape=(block, block), in_specs=[pl.BlockSpec(m...]
where the time goes in v3:
time: 94.8 us; the launch traced here: 94.6 us
  Pallas kernels  91 us (96%)
  local copies, waits for them, and re-layouts  2.95 us (3%)
    pallas_call x1, Pallas kernels, local(): pl.pallas_call(kernel, out_shape=(block, block), in_specs=[pl.BlockSpec(m...  91 us
    unnamed x2, local copies, waits for them, and re-layouts  2.95 us

profile of v3, /device:TPU:1, one launch (start us, length us, event | category | flops | bytes accessed | tf_op | source)
XLA Modules:
  0.0 94.6 jit_solution(5657529538506286970)
XLA Ops:
  0.6 91.0 %marchenko.1 = (bf16[8,32,128]{2,1,0:T(8,128)(2,1)}, bf16[8,32,128]{2,1,0:T(8,128)(2,1)}) custom-call(bf16[8,2,32,2048]{3,2,1,0:T(8,128)(2,1)} %refl_hbm.1, bf16[8,32,128]{2,1,0:T(8,128)(2,1)} %direct_hbm.1, s32[32,64]{1,0:T(8,128)} %onsets_hbm.1, bf16[512,512]{1,0:T(8,128)(2,1)} %constant.4.clone.first_hbm, bf16[4,128,512]{2,1,0:T(8,128)(2,1)} %constant.5.clone.second_hbm), custom_call_target="tpu_custom_call" | custom-call | tf_op jit(solution)/shard_map/marchenko/pallas_call | solution.py:348
  91.7 1.5 %copy.9 = bf16[8,32,128]{2,1,0:T(8,128)(2,1)} copy(bf16[8,32,128]{2,1,0:T(8,128)(2,1)} %get-tuple-element.4) | data formatting | bytes 131072
  93.1 1.5 %copy.10 = bf16[8,32,128]{2,1,0:T(8,128)(2,1)} copy(bf16[8,32,128]{2,1,0:T(8,128)(2,1)} %get-tuple-element.5) | data formatting | bytes 131072

commit v4 on v3

--- a/solution.py
+++ b/solution.py
@@ -348,7 +348,7 @@
     return pl.pallas_call(
         kernel,
         out_shape=(block, block),
-        in_specs=[pl.BlockSpec(memory_space=pl.ANY)] * 5,
+        in_specs=[pl.BlockSpec(memory_space=pltpu.HBM)] * 5,
         out_specs=(vmem, vmem),
         scratch_shapes=[
             pltpu.VMEM((8, 2, 32, 2048), BF),
@@ -379,9 +379,10 @@
             pltpu.SemaphoreType.DMA((ITERS, S, 6)),
         ],
         compiler_params=pltpu.CompilerParams(
-            collective_id=0, has_side_effects=True, vmem_limit_bytes=60 * 1024 * 1024),
+            collective_id=0, has_side_effects=True, vmem_limit_bytes=40 * 1024 * 1024),
         name="marchenko",
-    )(reflection, focus_direct, onsets, jnp.asarray(first), jnp.asarray(second))
+    )(*[pltpu.with_memory_space_constraint(a, pltpu.HBM)
+        for a in (reflection, focus_direct, onsets, jnp.asarray(first), jnp.asarray(second))])
 
 
 def solution(mesh):

time: 94.8 us -> 92.9 us (0.980)
  local copies, waits for them, and re-layouts: 2.95 us -> 1.26 us
    unnamed x2, local copies, waits for them, and re-layouts: 2.95 us -> 1.26 us
where the time goes in v4:
time: 92.9 us; the launch traced here: 92 us
  Pallas kernels  90.1 us (97%)
  local copies, waits for them, and re-layouts  1.26 us (1%)
    pallas_call x1, Pallas kernels, local(): pl.pallas_call(kernel, out_shape=(block, block), in_specs=[pl.BlockSpec(m...  90.1 us

profile of v4, /device:TPU:1, one launch (start us, length us, event | category | flops | bytes accessed | tf_op | source)
XLA Modules:
  0.0 92.0 jit_solution(4072635383623621978)
XLA Ops:
  0.6 90.1 %marchenko.1 = (bf16[8,32,128]{2,1,0:T(8,128)(2,1)S(1)}, bf16[8,32,128]{2,1,0:T(8,128)(2,1)S(1)}) custom-call(bf16[8,2,32,2048]{3,2,1,0:T(8,128)(2,1)} %refl_hbm.1, bf16[8,32,128]{2,1,0:T(8,128)(2,1)} %direct_hbm.1, s32[32,64]{1,0:T(8,128)} %onsets_hbm.1, bf16[512,512]{1,0:T(8,128)(2,1)} %constant.4.clone.first_hbm, ...), custom_call_target="tpu_custom_call" | custom-call | tf_op jit(solution)/shard_map/marchenko/pallas_call | solution.py:348
  90.7 0.6 copy.9
  91.4 0.6 copy.10

commit v5 on v4

--- a/solution.py
+++ b/solution.py
@@ -77,7 +77,7 @@
     def freq_on(d):
         return (wrap(fme + d), row)
 
-    around = [(du, dz) for du in (2, 1, 3, 0) for dz in (1, 0) if (du, dz) != (0, 0)]
+    around = [(du, dz) for dz in (1, 0) for du in (2, 1, 3, 0) if (du, dz) != (0, 0)]
     ring = [(d, cp) for d in (2, 1, 3) for cp in range(2)]
 
     bar = pltpu.get_barrier_semaphore()
@@ -313,6 +313,11 @@
             total(r2, it, s, xf2)
             for d in (2, 1, 3):
                 send_freq(xf2, it, s, d, 5).start()
+
+        @pl.when(it + 1 == ITERS)
+        def _():
+            unpack(minus.at[it], minus_out)
+
         for h in range(CHAINS):
             for s in range(h * Q, h * Q + Q):
                 all_freq(xf2, it, s, 5).wait_recv()
@@ -334,7 +339,6 @@
         return carry
 
     lax.fori_loop(0, ITERS, iteration, 0)
-    unpack(minus.at[ITERS - 1], minus_out)
     unpack(plus.at[ITERS], plus_out)
     for q in range(Q):
         all_reflection(q).wait_send()

time: 92.9 us -> 92.7 us (level)
  no operation moved by 1% of the time
where the time goes in v5:
time: 92.7 us; the launch traced here: 92.5 us
  Pallas kernels  90.6 us (98%)
  local copies, waits for them, and re-layouts  1.26 us (1%)
    pallas_call x1, Pallas kernels, local(): pl.pallas_call(kernel, out_shape=(block, block), in_specs=[pl.BlockSpec(m...  90.6 us

profile of v5, /device:TPU:1, one launch (start us, length us, event | category | flops | bytes accessed | tf_op | source)
XLA Modules:
  0.0 92.5 jit_solution(16494667285986514277)
XLA Ops:
  0.6 90.6 %marchenko.1 = (bf16[8,32,128]{2,1,0:T(8,128)(2,1)S(1)}, bf16[8,32,128]{2,1,0:T(8,128)(2,1)S(1)}) custom-call(bf16[8,2,32,2048]{3,2,1,0:T(8,128)(2,1)} %refl_hbm.1, bf16[8,32,128]{2,1,0:T(8,128)(2,1)} %direct_hbm.1, s32[32,64]{1,0:T(8,128)} %onsets_hbm.1, bf16[512,512]{1,0:T(8,128)(2,1)} %constant.4.clone.first_hbm, ...), custom_call_target="tpu_custom_call" | custom-call | tf_op jit(solution)/shard_map/marchenko/pallas_call | solution.py:352
  91.3 0.6 copy.9
  91.9 0.6 copy.10

commit v6 on v5

--- a/solution.py
+++ b/solution.py
@@ -332,14 +332,15 @@
                     for du, dz in around:
                         send_plus(it + 1, s, du, dz).start()
 
+        return carry
+
+    lax.fori_loop(0, ITERS, iteration, 0)
+    unpack(plus.at[ITERS], plus_out)
+    for it in range(ITERS):
         for s in range(S):
             for copies in (all_plus(it, s), all_rows(it, s), all_freq(xf1, it, s, 2), all_minus(it, s),
                            all_sources(it, s), all_freq(xf2, it, s, 5)):
                 copies.wait_send()
-        return carry
-
-    lax.fori_loop(0, ITERS, iteration, 0)
-    unpack(plus.at[ITERS], plus_out)
     for q in range(Q):
         all_reflection(q).wait_send()
 

time: 92.7 us -> 92.7 us (level)
  no operation moved by 1% of the time
where the time goes in v6:
time: 92.7 us; the launch traced here: 92.6 us
  Pallas kernels  90.7 us (98%)
  local copies, waits for them, and re-layouts  1.26 us (1%)
    pallas_call x1, Pallas kernels, local(): pl.pallas_call(kernel, out_shape=(block, block), in_specs=[pl.BlockSpec(m...  90.7 us

profile of v6, /device:TPU:1, one launch (start us, length us, event | category | flops | bytes accessed | tf_op | source)
XLA Modules:
  0.0 92.6 jit_solution(7518952551663343087)
XLA Ops:
  0.6 90.7 %marchenko.1 = (bf16[8,32,128]{2,1,0:T(8,128)(2,1)S(1)}, bf16[8,32,128]{2,1,0:T(8,128)(2,1)S(1)}) custom-call(bf16[8,2,32,2048]{3,2,1,0:T(8,128)(2,1)} %refl_hbm.1, bf16[8,32,128]{2,1,0:T(8,128)(2,1)} %direct_hbm.1, s32[32,64]{1,0:T(8,128)} %onsets_hbm.1, bf16[512,512]{1,0:T(8,128)(2,1)} %constant.4.clone.first_hbm, ...), custom_call_target="tpu_custom_call" | custom-call | tf_op jit(solution)/shard_map/marchenko/pallas_call | solution.py:353
  91.3 0.6 copy.9
  92.0 0.6 copy.10
